TPU v7x, 32 devices: a whole 2x2x4 slice. The times are simulated.
32 devices in a mesh: chan: 4 (over y, x), tile: 8 (over z, core).
Axes of the slice: x: 2, y: 2, z: 4, core: 2. Of those that a mesh axis runs over, the one named last changes fastest.
Arguments:
- voltages: bfloat16 [2, 32, 2048, 512], P(None, None, ('chan', 'tile')), may hold values from -6 to 6
- tile_pairs: int32 [528, 2], replicated, may hold values from 0 to 31, as said below
Outputs:
- visibilities: float32 [528, 32, 64, 128], P(None, ('chan', 'tile'))
Inputs may be any that keep to these rules, and one draw needn't show every extreme that they name: `tile_pairs`: every pair of panels (p, q) with p <= q occurs in exactly one row; in every row the first entry is at most the second.
All inputs are finite; a program needn't handle non-finite values.
Results may differ from a plain program's by a relative error of at most 0.0003.
Values may be sent and summed in bfloat16 or wider, within the bound.
A program may use at most 320 MiB of HBM per device.

v0:
```python
import jax
import jax.numpy as jnp
from jax import lax
from jax.sharding import PartitionSpec as P

PANELS = 32
TBLOCK = 128
PANEL = 64


def accumulate(running, turned):
    real_part = turned[0]
    imag_part = turned[1]
    left_all = jnp.concatenate((real_part, imag_part), axis=-1)
    rotated = jnp.concatenate((-imag_part, real_part), axis=-1)
    right_all = jnp.concatenate((left_all, rotated), axis=1)
    product = lax.dot_general(
        left_all, right_all, (((2,), (2,)), ((0,), (0,))), preferred_element_type=jnp.float32
    )
    return running + product


def body(voltages, tile_pairs):
    chans_here = voltages.shape[1] // (lax.axis_size("chan") * lax.axis_size("tile"))
    local_inputs = voltages.shape[2]
    spectra_all = voltages.shape[3]
    turn_count = spectra_all // TBLOCK
    inputs_all = PANELS * PANEL
    first_panel = tile_pairs[:, 0]
    second_panel = tile_pairs[:, 1]
    running = jnp.zeros((chans_here, inputs_all, 2 * inputs_all), jnp.float32)

    def advance(index, current):
        piece = lax.dynamic_slice_in_dim(voltages, index * TBLOCK, TBLOCK, 3)
        shaped = piece.reshape(2, voltages.shape[1], 1, local_inputs, TBLOCK)
        turned = lax.all_to_all(shaped, ("chan", "tile"), split_axis=1, concat_axis=2, tiled=True)
        turned = turned.reshape(2, chans_here, inputs_all, TBLOCK)
        return accumulate(current, turned)

    running = lax.fori_loop(0, turn_count, advance, running)
    grid = running.reshape(chans_here, PANELS, PANEL, 2, PANELS, PANEL)
    picked = grid[:, first_panel, :, :, second_panel, :]
    picked = picked.reshape(tile_pairs.shape[0], chans_here, PANEL, 2 * PANEL)
    return picked * spectra_all ** (-0.5)


def solution(mesh):
    placed = (P(None, None, ("chan", "tile"), None), P())
    return jax.shard_map(
        body,
        mesh=mesh,
        in_specs=placed,
        out_specs=P(None, ("chan", "tile"), None, None),
        check_vma=False,
    )
```

profile of v0, /device:TPU:9, one launch (start us, length us, event | category | flops | bytes accessed | tf_op | source)
XLA Modules:
  0.0 446.0 jit_solution(5651205347078184995)
XLA Ops:
  0.0 217.0 %while.14 = (s32[]{:T(128)}, f32[1,2048,4096]{2,1,0:T(8,128)}, bf16[2,32,64,512]{3,2,1,0:T(8,128)(2,1)}, s32[]{:T(128)}, s32[]{:T(128)}, /*index=5*/s32[]{:T(128)}, s32[]{:T(128)}) while((s32[]{:T(128)}, f32[1,2048,4096]{2,1,0:T(8,128)}, bf16[2,32,64,512]{3,2,1,0:T(8,128)(2,1)}, s32[]{:T(128)}, s32[]{:T(128)}, ...), condition=%wide.region_1.0_spmd.clone, body=%wide.region_0.0_spmd.clone.sunk | while | flops 4322492416 | bytes 77070504 | solution.py:40
  0.0 2.3 copy_bitcast_fusion.2
  2.3 6.4 %all-to-all-start = ((bf16[2,32,1,64,128]{4,3,0,2,1:T(8,128)(2,1)}), bf16[2,32,1,64,128]{4,3,0,2,1:T(8,128)(2,1)S(1)}, u32[]{:S(2)}, u32[]{:S(2)}) async-start(bf16[2,32,1,64,128]{4,3,0,2,1:T(8,128)(2,1)} %copy_bitcast_fusion.2), calls=%async_computation | async-start | bytes 2097152 | tf_op jit(solution)/shard_map/while/body/eval_jaxpr/all_to_all | solution.py:36
  8.7 24.1 %all-to-all-done = bf16[2,32,1,64,128]{4,3,0,2,1:T(8,128)(2,1)S(1)} async-done(((bf16[2,32,1,64,128]{4,3,0,2,1:T(8,128)(2,1)}), bf16[2,32,1,64,128]{4,3,0,2,1:T(8,128)(2,1)S(1)}, u32[]{:S(2)}, u32[]{:S(2)}) %all-to-all-start) | async-done | bytes 1048608 | tf_op jit(solution)/shard_map/while/body/eval_jaxpr/all_to_all | solution.py:36
  32.7 0.1 fusion.17
  32.8 0.1 neg.17
  32.9 13.1 %bitcast_add_fusion.2 = f32[1,2048,4096]{2,1,0:T(8,128)} fusion(f32[1,2048,4096]{2,1,0:T(8,128)} %get-tuple-element.127, pred[]{:T(512)S(6)} %compare.3, bf16[1,2048,128]{2,1,0:T(8,128)(2,1)S(1)} %bitcast.27, bf16[1,2048,128]{2,1,0:T(8,128)(2,1)S(1)} %neg.17, bf16[1,2048,128]{2,1,0:T(8,128)(2,1)S(1)} %bitcast.26), kind=kOutput, calls=%fused_computation.1.clone.1 | convolution fusion | flops 4322230272 | bytes 68681728 | tf_op jit(solution)/shard_map/while/body/eval_jaxpr/dot_general | solution.py:17
  46.0 2.3 copy_bitcast_fusion.2
  48.3 6.1 %all-to-all-start = ((bf16[2,32,1,64,128]{4,3,0,2,1:T(8,128)(2,1)}), bf16[2,32,1,64,128]{4,3,0,2,1:T(8,128)(2,1)S(1)}, u32[]{:S(2)}, u32[]{:S(2)}) async-start(bf16[2,32,1,64,128]{4,3,0,2,1:T(8,128)(2,1)} %copy_bitcast_fusion.2), calls=%async_computation | async-start | bytes 2097152 | tf_op jit(solution)/shard_map/while/body/eval_jaxpr/all_to_all | solution.py:36
  54.4 24.1 %all-to-all-done = bf16[2,32,1,64,128]{4,3,0,2,1:T(8,128)(2,1)S(1)} async-done(((bf16[2,32,1,64,128]{4,3,0,2,1:T(8,128)(2,1)}), bf16[2,32,1,64,128]{4,3,0,2,1:T(8,128)(2,1)S(1)}, u32[]{:S(2)}, u32[]{:S(2)}) %all-to-all-start) | async-done | bytes 1048608 | tf_op jit(solution)/shard_map/while/body/eval_jaxpr/all_to_all | solution.py:36
  78.6 0.1 fusion.17
  78.6 0.1 neg.17
  78.8 24.3 %bitcast_add_fusion.2 = f32[1,2048,4096]{2,1,0:T(8,128)} fusion(f32[1,2048,4096]{2,1,0:T(8,128)} %get-tuple-element.127, pred[]{:T(512)S(6)} %compare.3, bf16[1,2048,128]{2,1,0:T(8,128)(2,1)S(1)} %bitcast.27, bf16[1,2048,128]{2,1,0:T(8,128)(2,1)S(1)} %neg.17, bf16[1,2048,128]{2,1,0:T(8,128)(2,1)S(1)} %bitcast.26), kind=kOutput, calls=%fused_computation.1.clone.1 | convolution fusion | flops 4322230272 | bytes 68681728 | tf_op jit(solution)/shard_map/while/body/eval_jaxpr/dot_general | solution.py:17
  103.0 2.3 copy_bitcast_fusion.2
  105.3 6.1 %all-to-all-start = ((bf16[2,32,1,64,128]{4,3,0,2,1:T(8,128)(2,1)}), bf16[2,32,1,64,128]{4,3,0,2,1:T(8,128)(2,1)S(1)}, u32[]{:S(2)}, u32[]{:S(2)}) async-start(bf16[2,32,1,64,128]{4,3,0,2,1:T(8,128)(2,1)} %copy_bitcast_fusion.2), calls=%async_computation | async-start | bytes 2097152 | tf_op jit(solution)/shard_map/while/body/eval_jaxpr/all_to_all | solution.py:36
  111.4 24.1 %all-to-all-done = bf16[2,32,1,64,128]{4,3,0,2,1:T(8,128)(2,1)S(1)} async-done(((bf16[2,32,1,64,128]{4,3,0,2,1:T(8,128)(2,1)}), bf16[2,32,1,64,128]{4,3,0,2,1:T(8,128)(2,1)S(1)}, u32[]{:S(2)}, u32[]{:S(2)}) %all-to-all-start) | async-done | bytes 1048608 | tf_op jit(solution)/shard_map/while/body/eval_jaxpr/all_to_all | solution.py:36
  135.5 0.1 fusion.17
  135.6 0.1 neg.17
  135.7 24.3 %bitcast_add_fusion.2 = f32[1,2048,4096]{2,1,0:T(8,128)} fusion(f32[1,2048,4096]{2,1,0:T(8,128)} %get-tuple-element.127, pred[]{:T(512)S(6)} %compare.3, bf16[1,2048,128]{2,1,0:T(8,128)(2,1)S(1)} %bitcast.27, bf16[1,2048,128]{2,1,0:T(8,128)(2,1)S(1)} %neg.17, bf16[1,2048,128]{2,1,0:T(8,128)(2,1)S(1)} %bitcast.26), kind=kOutput, calls=%fused_computation.1.clone.1 | convolution fusion | flops 4322230272 | bytes 68681728 | tf_op jit(solution)/shard_map/while/body/eval_jaxpr/dot_general | solution.py:17
  160.0 2.3 copy_bitcast_fusion.2
  162.3 6.1 %all-to-all-start = ((bf16[2,32,1,64,128]{4,3,0,2,1:T(8,128)(2,1)}), bf16[2,32,1,64,128]{4,3,0,2,1:T(8,128)(2,1)S(1)}, u32[]{:S(2)}, u32[]{:S(2)}) async-start(bf16[2,32,1,64,128]{4,3,0,2,1:T(8,128)(2,1)} %copy_bitcast_fusion.2), calls=%async_computation | async-start | bytes 2097152 | tf_op jit(solution)/shard_map/while/body/eval_jaxpr/all_to_all | solution.py:36
  168.4 24.1 %all-to-all-done = bf16[2,32,1,64,128]{4,3,0,2,1:T(8,128)(2,1)S(1)} async-done(((bf16[2,32,1,64,128]{4,3,0,2,1:T(8,128)(2,1)}), bf16[2,32,1,64,128]{4,3,0,2,1:T(8,128)(2,1)S(1)}, u32[]{:S(2)}, u32[]{:S(2)}) %all-to-all-start) | async-done | bytes 1048608 | tf_op jit(solution)/shard_map/while/body/eval_jaxpr/all_to_all | solution.py:36
  192.5 0.1 fusion.17
  192.6 0.1 neg.17
  192.7 24.3 %bitcast_add_fusion.2 = f32[1,2048,4096]{2,1,0:T(8,128)} fusion(f32[1,2048,4096]{2,1,0:T(8,128)} %get-tuple-element.127, pred[]{:T(512)S(6)} %compare.3, bf16[1,2048,128]{2,1,0:T(8,128)(2,1)S(1)} %bitcast.27, bf16[1,2048,128]{2,1,0:T(8,128)(2,1)S(1)} %neg.17, bf16[1,2048,128]{2,1,0:T(8,128)(2,1)S(1)} %bitcast.26), kind=kOutput, calls=%fused_computation.1.clone.1 | convolution fusion | flops 4322230272 | bytes 68681728 | tf_op jit(solution)/shard_map/while/body/eval_jaxpr/dot_general | solution.py:17
  217.0 52.7 %reshape.66 = f32[32,64,2,32,64]{4,3,2,1,0:T(8,128)} reshape(f32[1,2048,4096]{2,1,0:T(8,128)} %get-tuple-element.69) | data formatting | bytes 67108864 | tf_op jit(solution)/shard_map/reshape | solution.py:41
  269.6 56.3 %copy.13 = f32[32,64,2,32,64]{4,1,3,2,0:T(8,128)} copy(f32[32,64,2,32,64]{4,3,2,1,0:T(8,128)} %reshape.66) | data formatting | bytes 67108864 | tf_op jit(solution)/shard_map/reshape | solution.py:41
  325.9 0.0 copy-done
  326.0 50.4 %gather_fusion = f32[528,64,2,64]{3,1,2,0:T(8,128)} fusion(f32[32,64,2,32,64]{4,1,3,2,0:T(8,128)} %copy.13, s32[528]{0:T(1024)S(1)} %fusion.14), kind=kCustom, calls=%fused_computation | custom fusion | bytes 34607232 | tf_op jit(solution)/shard_map/gather | solution.py:42
  376.4 32.3 %copy.14 = f32[528,64,2,64]{0,3,2,1:T(8,128)} copy(f32[528,64,2,64]{3,1,2,0:T(8,128)} %gather_fusion) | data formatting | bytes 34603008 | tf_op jit(solution)/shard_map/gather | solution.py:42
  408.7 17.3 %broadcast_multiply_fusion = f32[528,64,2,64]{0,3,2,1:T(8,128)} fusion(f32[528,64,2,64]{0,3,2,1:T(8,128)} %copy.14), kind=kLoop, calls=%fused_computation.15 | loop fusion | flops 4325376 | bytes 34603008 | tf_op jit(solution)/shard_map/mul | solution.py:44
  426.0 19.9 %copy.15 = f32[528,1,64,128]{3,2,1,0:T(8,128)} copy(f32[528,1,64,128]{0,3,2,1:T(8,128)} %bitcast.28) | data formatting | bytes 34603008 | tf_op jit(solution)/shard_map/mul | solution.py:44
  (3 shorter events, 0.0 us)
Async XLA Ops:
  2.3 30.4 %all-to-all-start = ((bf16[2,32,1,64,128]{4,3,0,2,1:T(8,128)(2,1)}), bf16[2,32,1,64,128]{4,3,0,2,1:T(8,128)(2,1)S(1)}, u32[]{:S(2)}, u32[]{:S(2)}) async-start(bf16[2,32,1,64,128]{4,3,0,2,1:T(8,128)(2,1)} %copy_bitcast_fusion.2), calls=%async_computation | async-start | bytes 2097152 | tf_op jit(solution)/shard_map/while/body/eval_jaxpr/all_to_all | solution.py:36
  48.3 30.2 %all-to-all-start = ((bf16[2,32,1,64,128]{4,3,0,2,1:T(8,128)(2,1)}), bf16[2,32,1,64,128]{4,3,0,2,1:T(8,128)(2,1)S(1)}, u32[]{:S(2)}, u32[]{:S(2)}) async-start(bf16[2,32,1,64,128]{4,3,0,2,1:T(8,128)(2,1)} %copy_bitcast_fusion.2), calls=%async_computation | async-start | bytes 2097152 | tf_op jit(solution)/shard_map/while/body/eval_jaxpr/all_to_all | solution.py:36
  105.3 30.2 %all-to-all-start = ((bf16[2,32,1,64,128]{4,3,0,2,1:T(8,128)(2,1)}), bf16[2,32,1,64,128]{4,3,0,2,1:T(8,128)(2,1)S(1)}, u32[]{:S(2)}, u32[]{:S(2)}) async-start(bf16[2,32,1,64,128]{4,3,0,2,1:T(8,128)(2,1)} %copy_bitcast_fusion.2), calls=%async_computation | async-start | bytes 2097152 | tf_op jit(solution)/shard_map/while/body/eval_jaxpr/all_to_all | solution.py:36
  162.3 30.2 %all-to-all-start = ((bf16[2,32,1,64,128]{4,3,0,2,1:T(8,128)(2,1)}), bf16[2,32,1,64,128]{4,3,0,2,1:T(8,128)(2,1)S(1)}, u32[]{:S(2)}, u32[]{:S(2)}) async-start(bf16[2,32,1,64,128]{4,3,0,2,1:T(8,128)(2,1)} %copy_bitcast_fusion.2), calls=%async_computation | async-start | bytes 2097152 | tf_op jit(solution)/shard_map/while/body/eval_jaxpr/all_to_all | solution.py:36
  269.6 56.3 %copy-start = (s32[528,2]{0,1:T(2,128)S(1)}, s32[528,2]{0,1:T(2,128)}, u32[]{:S(2)}) copy-start(s32[528,2]{0,1:T(2,128)} %param.5) | copy-start | bytes 12676
where the time goes:
time: 453 us; the launch traced here: 446 us
  local copies, waits for them, and re-layouts  221 us (49%)
  waiting for transfers between devices  96.4 us (21%)
  matrix products  85.9 us (19%)
  starting transfers between devices  24.7 us (5%)
  other arithmetic  17.8 us (4%)
    reshape x2, local copies, waits for them, and re-layouts, body(): grid = running.reshape(chans_here, PANELS, PANEL, 2, PANELS, PANEL)  109 us
    all_to_all x4, waiting for transfers between devices, advance(): lax.all_to_all(shaped, ('chan', 'tile'), split_axis=1, concat_axis=2, til...  96.4 us
    dot_general x4, matrix products, accumulate(): lax.dot_general(left_all, right_all, (((2,), (2,)), ((0,), (0,))), prefer...  85.9 us
    gather x2, local copies, waits for them, and re-layouts, body(): picked = grid[:, first_panel, :, :, second_panel, :]  82.7 us
    all_to_all x4, starting transfers between devices, advance(): lax.all_to_all(shaped, ('chan', 'tile'), split_axis=1, concat_axis=2, til...  24.7 us
    mul x1, local copies, waits for them, and re-layouts, body(): return picked * spectra_all ** (-0.5)  19.9 us
    mul x1, other arithmetic, body(): return picked * spectra_all ** (-0.5)  17.3 us
    reshape x4, local copies, waits for them, and re-layouts, advance(): shaped = piece.reshape(2, voltages.shape[1], 1, local_inputs, TBLOCK)  9.15 us
  transfers between devices with their start and end apart: 4, of which 4 were waited for; matrix products, arithmetic and copies ran while one was open for 0% of the time, Pallas kernels for 0%

commit v1 on v0

v1 whole, which is shorter than its diff:
```python
import functools

import jax
import jax.numpy as jnp
from jax import lax
from jax.experimental import pallas as pl
from jax.experimental.pallas import tpu as pltpu
from jax.sharding import PartitionSpec as P

PANELS = 32
PANEL = 64
GROUP = 4
GROUPS = PANELS // GROUP
MESH = pl.DeviceIdType.MESH


def flipped(index, mask):
    for bit in range(mask.bit_length()):
        if mask >> bit & 1:
            index = index + (1 << bit) * (1 - 2 * (index // (1 << bit) % 2))
    return index


def send_order(chan_size, tile_size):
    half = tile_size // 2
    order = []
    for chan_mask in range(chan_size):
        for tile_mask in range(half):
            order.append((chan_mask, tile_mask + half))
            if chan_mask or tile_mask:
                order.append((chan_mask, tile_mask))
    return order


def turn_kernel(sizes, pairs_ref, volt_ref, turned_ref, slots_ref, send_sem, recv_sem, own_sem):
    chan_size, tile_size = sizes
    chan, tile = lax.axis_index("chan"), lax.axis_index("tile")
    me = chan * tile_size + tile
    inputs = volt_ref.shape[2]
    here = turned_ref.shape[1]
    order = send_order(chan_size, tile_size)

    barrier = pltpu.get_barrier_semaphore()
    for masks in order:
        to = (flipped(chan, masks[0]), flipped(tile, masks[1]))
        pl.semaphore_signal(barrier, inc=1, device_id=to, device_id_type=MESH)
    pl.semaphore_wait(barrier, len(order))

    rows = pl.ds(pl.multiple_of(me * inputs, inputs), inputs)
    own = pltpu.make_async_copy(volt_ref.at[:, pl.ds(me * here, here)], turned_ref.at[:, :, rows], own_sem)
    copies = []
    for masks in order:
        to = (flipped(chan, masks[0]), flipped(tile, masks[1]))
        flat = to[0] * tile_size + to[1]
        copies.append(
            pltpu.make_async_remote_copy(
                src_ref=volt_ref.at[:, pl.ds(flat * here, here)],
                dst_ref=turned_ref.at[:, :, rows],
                send_sem=send_sem.at[len(copies)],
                recv_sem=recv_sem.at[len(copies)],
                device_id=to,
                device_id_type=MESH,
            )
        )
        copies[-1].start()
    own.start()

    code = pairs_ref[:, 0:1] * PANELS + pairs_ref[:, 1:2]
    slot = lax.broadcasted_iota(jnp.int32, (code.shape[0], 128), 0)
    for part in range(PANELS * PANELS // 128):
        wanted = lax.broadcasted_iota(jnp.int32, (code.shape[0], 128), 1) + part * 128
        slots_ref[:, part * 128 : part * 128 + 128] = jnp.sum(
            jnp.where(code == wanted, slot, 0), axis=0, keepdims=True
        )

    own.wait()
    for copy in copies:
        copy.wait()


def product_kernel(slots_ref, turned_ref, out_ref, left, right, stage, load_sem, out_sem):
    here, spectra = turned_ref.shape[1], turned_ref.shape[3]
    width = GROUP * PANEL
    scale = spectra ** (-0.5)
    for f in range(here):
        loads = []
        for g in range(GROUPS):
            rows = pl.ds(g * width, width)
            for part in range(2):
                loads.append(
                    pltpu.make_async_copy(
                        turned_ref.at[part, f, rows],
                        left.at[rows, pl.ds(part * spectra, spectra)],
                        load_sem.at[2 * g + part],
                    )
                )
                loads[-1].start()
        for h in range(GROUPS):
            loads[2 * h].wait()
            loads[2 * h + 1].wait()
            for q in range(GROUP):
                first = (h * GROUP + q) * PANEL
                real_part = left[first : first + PANEL, :spectra]
                imag_part = left[first : first + PANEL, spectra:]
                right[q * 2 * PANEL : q * 2 * PANEL + PANEL, :spectra] = real_part
                right[q * 2 * PANEL : q * 2 * PANEL + PANEL, spectra:] = imag_part
                right[q * 2 * PANEL + PANEL : (q + 1) * 2 * PANEL, :spectra] = -imag_part
                right[q * 2 * PANEL + PANEL : (q + 1) * 2 * PANEL, spectra:] = real_part

            def block(g, carry):
                at = h * (h + 1) // 2 + g
                product = (
                    lax.dot_general(
                        left[pl.ds(pl.multiple_of(g * width, width), width), :],
                        right[...],
                        (((1,), (1,)), ((), ())),
                        preferred_element_type=jnp.float32,
                    )
                    * scale
                )
                for m in range(GROUP):
                    for q in range(GROUP):
                        stage[at, m * GROUP + q] = product[
                            m * PANEL : (m + 1) * PANEL, q * 2 * PANEL : (q + 1) * 2 * PANEL
                        ]
                for m in range(GROUP):
                    for q in range(GROUP):

                        def put():
                            slot = slots_ref[0, (g * GROUP + m) * PANELS + h * GROUP + q]
                            pltpu.make_async_copy(stage.at[at, m * GROUP + q], out_ref.at[slot, f], out_sem).start()

                        if m <= q:
                            put()
                        else:
                            pl.when(g < h)(put)
                return carry

            lax.fori_loop(0, h + 1, block, 0)

        def drain(index, carry):
            pltpu.make_async_copy(stage.at[0], stage.at[0], out_sem).wait()
            return carry

        lax.fori_loop(0, PANELS * (PANELS + 1) // 2 // (GROUP * GROUP), drain, 0)


def body(sizes, voltages, tile_pairs):
    chan_size, tile_size = sizes
    parts, chans, inputs, spectra = voltages.shape
    here = chans // (chan_size * tile_size)
    all_inputs = PANELS * PANEL
    count = chan_size * tile_size - 1
    pairs = tile_pairs.shape[0]
    turned, slots = pl.pallas_call(
        functools.partial(turn_kernel, sizes),
        out_shape=(
            jax.ShapeDtypeStruct((parts, here, all_inputs, spectra), voltages.dtype),
            jax.ShapeDtypeStruct((1, PANELS * PANELS), jnp.int32),
        ),
        in_specs=[pl.BlockSpec(memory_space=pltpu.VMEM), pl.BlockSpec(memory_space=pl.ANY)],
        out_specs=(pl.BlockSpec(memory_space=pl.ANY), pl.BlockSpec(memory_space=pltpu.VMEM)),
        scratch_shapes=[
            pltpu.SemaphoreType.DMA((count,)),
            pltpu.SemaphoreType.DMA((count,)),
            pltpu.SemaphoreType.DMA,
        ],
        compiler_params=pltpu.CompilerParams(
            collective_id=0, has_side_effects=True, vmem_limit_bytes=32 * 1024 * 1024
        ),
        name="corner_turn",
    )(tile_pairs, voltages)
    width = GROUP * PANEL
    return pl.pallas_call(
        product_kernel,
        out_shape=jax.ShapeDtypeStruct((pairs, here, PANEL, 2 * PANEL), jnp.float32),
        in_specs=[pl.BlockSpec(memory_space=pltpu.SMEM), pl.BlockSpec(memory_space=pl.ANY)],
        out_specs=pl.BlockSpec(memory_space=pl.ANY),
        scratch_shapes=[
            pltpu.VMEM((all_inputs, parts * spectra), voltages.dtype),
            pltpu.VMEM((2 * width, parts * spectra), voltages.dtype),
            pltpu.VMEM((GROUPS * (GROUPS + 1) // 2, GROUP * GROUP, PANEL, 2 * PANEL), jnp.float32),
            pltpu.SemaphoreType.DMA((2 * GROUPS,)),
            pltpu.SemaphoreType.DMA,
        ],
        compiler_params=pltpu.CompilerParams(vmem_limit_bytes=48 * 1024 * 1024),
        name="tile_products",
    )(slots, turned)


def solution(mesh):
    sizes = (mesh.shape["chan"], mesh.shape["tile"])
    return jax.shard_map(
        functools.partial(body, sizes),
        mesh=mesh,
        in_specs=(P(None, None, ("chan", "tile"), None), P()),
        out_specs=P(None, ("chan", "tile"), None, None),
        check_vma=False,
    )
```

time: 453 us -> 122 us (0.27); the launches traced: 446 us -> 122 us
  local copies, waits for them, and re-layouts: 221 us -> 3.01 us
  Pallas kernels: 0 us -> 119 us
  waiting for transfers between devices: 96.4 us -> 0 us
  matrix products: 85.9 us -> 0 us
  starting transfers between devices: 24.7 us -> 0 us
  other arithmetic: 17.8 us -> 0 us
    pallas_call x0 -> x2, Pallas kernels: none -> 119 us  [the longest x1 99.7 us: body(): pl.pallas_call(functools.partial(turn_kernel, sizes), out_shape=(jax.Shap...]
    reshape x6 -> x0, local copies, waits for them, and re-layouts: 118 us -> none  [the longest x2 109 us: body(): grid = running.reshape(chans_here, PANELS, PANEL, 2, PANELS, PANEL)]
    all_to_all x4 -> x0, waiting for transfers between devices: 96.4 us -> none  [advance(): lax.all_to_all(shaped, ('chan', 'tile'), split_axis=1, concat_axis=2, til...]
    dot_general x4 -> x0, matrix products: 85.9 us -> none  [accumulate(): lax.dot_general(left_all, right_all, (((2,), (2,)), ((0,), (0,))), prefer...]
    gather x2 -> x0, local copies, waits for them, and re-layouts: 82.7 us -> none  [body(): picked = grid[:, first_panel, :, :, second_panel, :]]
    all_to_all x4 -> x0, starting transfers between devices: 24.7 us -> none  [advance(): lax.all_to_all(shaped, ('chan', 'tile'), split_axis=1, concat_axis=2, til...]
    mul x1 -> x0, local copies, waits for them, and re-layouts: 19.9 us -> none  [body(): return picked * spectra_all ** (-0.5)]
    mul x1 -> x0, other arithmetic: 17.3 us -> none  [body(): return picked * spectra_all ** (-0.5)]
  transfers between devices with their start and end apart: 4 -> 0, of which waited for: 4 -> 0; matrix products, arithmetic and copies ran while one was open for 0% -> 0% of each run, Pallas kernels for 0% -> 0%
where the time goes in v1:
time: 122 us
  Pallas kernels  119 us (98%)
  local copies, waits for them, and re-layouts  3.01 us (2%)
    pallas_call x1, Pallas kernels, body(): pl.pallas_call(functools.partial(turn_kernel, sizes), out_shape=(jax.Shap...  99.7 us
    pallas_call x1, Pallas kernels, body(): pl.pallas_call(product_kernel, out_shape=jax.ShapeDtypeStruct((pairs, her...  19.6 us
    unnamed x3, local copies, waits for them, and re-layouts  3.01 us

profile of v1, /device:TPU:9, one launch (start us, length us, event | category | flops | bytes accessed | tf_op | source)
XLA Modules:
  0.0 122.3 jit_solution(7215883937491961844)
XLA Ops:
  0.0 0.8 copy.3.pairs_ref
  0.8 0.0 copy-start
  0.8 2.2 %copy-done = bf16[2,32,64,512]{3,2,1,0:T(8,128)(2,1)S(1)} copy-done((bf16[2,32,64,512]{3,2,1,0:T(8,128)(2,1)S(1)}, bf16[2,32,64,512]{3,2,1,0:T(8,128)(2,1)}, u32[]{:S(2)}) %copy-start) | copy-done | bytes 4194328
  3.0 99.7 %corner_turn.1 = (bf16[2,1,2048,512]{3,2,1,0:T(8,128)(2,1)S(1)}, s32[1,1024]{1,0:T(1,128)S(1)}) custom-call(s32[528,2]{1,0:T(8,128)S(1)} %copy.3.pairs_ref, bf16[2,32,64,512]{3,2,1,0:T(8,128)(2,1)S(1)} %copy-done), custom_call_target="tpu_custom_call" | custom-call | tf_op jit(solution)/shard_map/corner_turn/pallas_call | solution.py:155
  102.7 19.6 %tile_products.1 = f32[528,1,64,128]{3,2,1,0:T(8,128)} custom-call(s32[1,1024]{1,0:T(1,128)S(1)} %get-tuple-element.7.slots_ref, bf16[2,1,2048,512]{3,2,1,0:T(8,128)(2,1)S(1)} %get-tuple-element.8.turned_ref), custom_call_target="tpu_custom_call" | custom-call | tf_op jit(solution)/shard_map/tile_products/pallas_call | solution.py:174
Async XLA Ops:
  0.8 2.2 %copy-start = (bf16[2,32,64,512]{3,2,1,0:T(8,128)(2,1)S(1)}, bf16[2,32,64,512]{3,2,1,0:T(8,128)(2,1)}, u32[]{:S(2)}) copy-start(bf16[2,32,64,512]{3,2,1,0:T(8,128)(2,1)} %volt_ref.1) | copy-start | bytes 12582916

commit v2 on v0

v2 whole, which is shorter than its diff:
```python
import functools

import jax
import jax.numpy as jnp
from jax import lax
from jax.experimental import pallas as pl
from jax.experimental.pallas import tpu as pltpu
from jax.sharding import PartitionSpec as P

PANELS = 32
PANEL = 64
LATE = 1
MESH = pl.DeviceIdType.MESH
MIB = 1024 * 1024


def flipped(index, mask, size):
    bit, result = 1, 0
    while bit < size:
        result = result + (index // bit + mask // bit) % 2 * bit
        bit *= 2
    return result


def group_at(sizes, chan, tile, place):
    half = sizes[1] // 2
    return flipped(chan, place // 2, sizes[0]) * 2 + (tile // half + place) % 2


def pair_index(a, b):
    count = lambda groups: groups * (groups - 1) // 2
    return count(b) + a


def send_order(sizes):
    half = sizes[1] // 2
    order = []
    for chan_mask in range(sizes[0]):
        for tile_mask in range(half):
            order.append((chan_mask, tile_mask + half))
            if chan_mask or tile_mask:
                order.append((chan_mask, tile_mask))
    return order


def multiply(turned_ref, right_ref, store, g, h, width):
    spectra = turned_ref.shape[3]
    rows = pl.ds(pl.multiple_of(g * width, width), width)
    total = None
    for part in range(2):
        term = lax.dot_general(
            turned_ref[part, 0, rows, :],
            right_ref[h, part],
            (((1,), (1,)), ((), ())),
            preferred_element_type=jnp.float32,
        )
        total = term if total is None else total + term
    total = total * spectra ** (-0.5)
    per = width // PANEL
    for m in range(per):
        for q in range(per):
            store(m * per + q, total[m * PANEL : (m + 1) * PANEL, q * 2 * PANEL : (q + 1) * 2 * PANEL])


def turn_kernel(
    sizes, pairs_ref, volt_ref, turned_ref, right_ref, tiles_ref, slots_ref, send_sem, recv_sem, own_sem
):
    chan, tile = lax.axis_index("chan"), lax.axis_index("tile")
    me = chan * sizes[1] + tile
    inputs = volt_ref.shape[2]
    groups = 2 * sizes[0]
    width = turned_ref.shape[2] // groups
    per = width // PANEL
    order = send_order(sizes)

    barrier = pltpu.get_barrier_semaphore()
    for masks in order:
        to = (flipped(chan, masks[0], sizes[0]), flipped(tile, masks[1], sizes[1]))
        pl.semaphore_signal(barrier, inc=1, device_id=to, device_id_type=MESH)
    pl.semaphore_wait(barrier, len(order))

    rows = pl.ds(pl.multiple_of(me * inputs, inputs), inputs)
    copies = {}
    for number, masks in enumerate(order):
        to = (flipped(chan, masks[0], sizes[0]), flipped(tile, masks[1], sizes[1]))
        copies[masks] = pltpu.make_async_remote_copy(
            src_ref=volt_ref.at[:, pl.ds(to[0] * sizes[1] + to[1], 1)],
            dst_ref=turned_ref.at[:, :, rows],
            send_sem=send_sem.at[number],
            recv_sem=recv_sem.at[number],
            device_id=to,
            device_id_type=MESH,
        )
        copies[masks].start()
    own = pltpu.make_async_copy(volt_ref.at[:, pl.ds(me, 1)], turned_ref.at[:, :, rows], own_sem)
    own.start()

    listed = pairs_ref.shape[1]
    code = pairs_ref[0:1, :] * PANELS + pairs_ref[1:2, :]
    code = jnp.transpose(jnp.broadcast_to(code, (128, listed)))
    slot = lax.broadcasted_iota(jnp.int32, (listed, 128), 0)
    lane = lax.broadcasted_iota(jnp.int32, (listed, 128), 1)
    for part in range(PANELS * PANELS // 128):
        slots_ref[:, part * 128 : part * 128 + 128] = jnp.sum(
            jnp.where(code == lane + part * 128, slot, 0), axis=0, keepdims=True
        )

    own.wait()
    for place in range(groups):
        for masks in order:
            if masks[0] * 2 + masks[1] // (sizes[1] // 2) == place:
                copies[masks].wait_recv()
        x = group_at(sizes, chan, tile, place)
        for q in range(per):
            panel = pl.ds(pl.multiple_of(x * width + q * PANEL, PANEL), PANEL)
            real_part = turned_ref[0, 0, panel, :]
            imag_part = turned_ref[1, 0, panel, :]
            first, second = pl.ds(q * 2 * PANEL, PANEL), pl.ds(q * 2 * PANEL + PANEL, PANEL)
            right_ref[x, 0, first, :] = real_part
            right_ref[x, 0, second, :] = -imag_part
            right_ref[x, 1, first, :] = imag_part
            right_ref[x, 1, second, :] = real_part
        if place < groups - LATE:

            def block(other, carry):
                y = group_at(sizes, chan, tile, other)
                at = jnp.where(other == place, pair_index(0, groups - LATE) + place, pair_index(other, place))

                def store(number, value):
                    tiles_ref[at, number] = value

                multiply(turned_ref, right_ref, store, jnp.minimum(x, y), jnp.maximum(x, y), width)
                return carry

            lax.fori_loop(0, place + 1, block, 0)

    for masks in order:
        copies[masks].wait_send()


def place_kernel(sizes, slots_ref, turned_ref, right_ref, tiles_ref, out_ref, last_ref, sem):
    chan, tile = lax.axis_index("chan"), lax.axis_index("tile")
    groups = 2 * sizes[0]
    width = turned_ref.shape[2] // groups
    per = width // PANEL
    early = groups - LATE

    def put(source, x, y):
        g, h = (x, y) if x is y else (jnp.minimum(x, y), jnp.maximum(x, y))
        base = g * (per * PANELS) + h * per
        for m in range(per):
            for q in range(m if x is y else 0, per):
                slot = slots_ref[0, base + m * PANELS + q]
                pltpu.make_async_copy(source.at[m * per + q], out_ref.at[slot, 0], sem).start()

    ids = [group_at(sizes, chan, tile, place) for place in range(groups)]
    ready = [(a, b) for b in range(early) for a in range(b)]
    ready += [(a, a) for a in range(early)]
    late = [(a, b) for b in range(early, groups) for a in range(b + 1)]
    share = -(-len(ready) // len(late))
    for number, (a, b) in enumerate(late):
        for k in range(number * share, min((number + 1) * share, len(ready))):
            put(tiles_ref.at[k], ids[ready[k][0]], ids[ready[k][1]])

        def store(place, value):
            last_ref[number, place] = value

        multiply(
            turned_ref, right_ref, store, jnp.minimum(ids[a], ids[b]), jnp.maximum(ids[a], ids[b]), width
        )
        put(last_ref.at[number], ids[a], ids[b])

    def drain(index, carry):
        pltpu.make_async_copy(last_ref.at[0], last_ref.at[0], sem).wait()
        return carry

    lax.fori_loop(0, out_ref.shape[0] // (per * per), drain, 0)


def body(sizes, voltages, tile_pairs):
    parts, chans, inputs, spectra = voltages.shape
    devices = sizes[0] * sizes[1]
    groups = 2 * sizes[0]
    per = PANELS // groups
    listed = tile_pairs.shape[0]
    if chans != devices or listed % (per * per):
        raise ValueError("unsupported sizes")
    early = groups - LATE
    vmem = pl.BlockSpec(memory_space=pltpu.VMEM)
    results = pl.pallas_call(
        functools.partial(turn_kernel, sizes),
        out_shape=(
            pltpu.VMEM((parts, 1, PANELS * PANEL, spectra), voltages.dtype),
            pltpu.VMEM((groups, 2, 2 * per * PANEL, spectra), voltages.dtype),
            pltpu.VMEM((early * (early + 1) // 2, per * per, PANEL, 2 * PANEL), jnp.float32),
            pltpu.VMEM((1, PANELS * PANELS), jnp.int32),
        ),
        in_specs=[vmem, pl.BlockSpec(memory_space=pltpu.HBM)],
        out_specs=(vmem,) * 4,
        scratch_shapes=[
            pltpu.SemaphoreType.DMA((devices - 1,)),
            pltpu.SemaphoreType.DMA((devices - 1,)),
            pltpu.SemaphoreType.DMA,
        ],
        compiler_params=pltpu.CompilerParams(
            collective_id=0, has_side_effects=True, vmem_limit_bytes=12 * MIB
        ),
        name="corner_turn",
    )(tile_pairs.T, pltpu.with_memory_space_constraint(voltages, pltpu.HBM))
    turned, right, tiles, slots = results
    return pl.pallas_call(
        functools.partial(place_kernel, sizes),
        out_shape=jax.ShapeDtypeStruct((listed, 1, PANEL, 2 * PANEL), jnp.float32),
        in_specs=[pl.BlockSpec(memory_space=pltpu.SMEM), vmem, vmem, vmem],
        out_specs=pl.BlockSpec(memory_space=pl.ANY),
        scratch_shapes=[
            pltpu.VMEM((groups * LATE - LATE * (LATE - 1) // 2, per * per, PANEL, 2 * PANEL), jnp.float32),
            pltpu.SemaphoreType.DMA,
        ],
        compiler_params=pltpu.CompilerParams(vmem_limit_bytes=16 * MIB),
        name="tile_placement",
    )(slots, turned, right, tiles)


def solution(mesh):
    sizes = (mesh.shape["chan"], mesh.shape["tile"])
    return jax.shard_map(
        functools.partial(body, sizes),
        mesh=mesh,
        in_specs=(P(None, None, ("chan", "tile"), None), P()),
        out_specs=P(None, ("chan", "tile"), None, None),
        check_vma=False,
    )
```

time: 453 us -> 108 us (0.24); the launches traced: 446 us -> 108 us
  local copies, waits for them, and re-layouts: 221 us -> 0.69 us
  Pallas kernels: 0 us -> 107 us
  waiting for transfers between devices: 96.4 us -> 0 us
  matrix products: 85.9 us -> 0 us
  starting transfers between devices: 24.7 us -> 0 us
  other arithmetic: 17.8 us -> 0 us
    reshape x6 -> x0, local copies, waits for them, and re-layouts: 118 us -> none  [the longest x2 109 us: body(): grid = running.reshape(chans_here, PANELS, PANEL, 2, PANELS, PANEL)]
    pallas_call x0 -> x2, Pallas kernels: none -> 107 us  [the longest x1 100 us: body(): pl.pallas_call(functools.partial(turn_kernel, sizes), out_shape=(pltpu.VM...]
    all_to_all x4 -> x0, waiting for transfers between devices: 96.4 us -> none  [advance(): lax.all_to_all(shaped, ('chan', 'tile'), split_axis=1, concat_axis=2, til...]
    dot_general x4 -> x0, matrix products: 85.9 us -> none  [accumulate(): lax.dot_general(left_all, right_all, (((2,), (2,)), ((0,), (0,))), prefer...]
    gather x2 -> x0, local copies, waits for them, and re-layouts: 82.7 us -> none  [body(): picked = grid[:, first_panel, :, :, second_panel, :]]
    all_to_all x4 -> x0, starting transfers between devices: 24.7 us -> none  [advance(): lax.all_to_all(shaped, ('chan', 'tile'), split_axis=1, concat_axis=2, til...]
    mul x1 -> x0, local copies, waits for them, and re-layouts: 19.9 us -> none  [body(): return picked * spectra_all ** (-0.5)]
    mul x1 -> x0, other arithmetic: 17.3 us -> none  [body(): return picked * spectra_all ** (-0.5)]
  transfers between devices with their start and end apart: 4 -> 0, of which waited for: 4 -> 0; matrix products, arithmetic and copies ran while one was open for 0% -> 0% of each run, Pallas kernels for 0% -> 0%
where the time goes in v2:
time: 108 us
  Pallas kernels  107 us (99%)
    pallas_call x1, Pallas kernels, body(): pl.pallas_call(functools.partial(turn_kernel, sizes), out_shape=(pltpu.VM...  100 us
    pallas_call x1, Pallas kernels, body(): pl.pallas_call(functools.partial(place_kernel, sizes), out_shape=jax.Shap...  6.9 us

profile of v2, /device:TPU:9, one launch (start us, length us, event | category | flops | bytes accessed | tf_op | source)
XLA Modules:
  0.0 107.6 jit_solution(12488651204085869853)
XLA Ops:
  0.0 0.0 copy-start
  0.0 0.7 copy-done
  0.7 100.0 %corner_turn.1 = (bf16[2,1,2048,512]{3,2,1,0:T(8,128)(2,1)S(1)}, bf16[8,2,512,512]{3,2,1,0:T(8,128)(2,1)S(1)}, f32[28,16,64,128]{3,2,1,0:T(8,128)S(1)}, s32[1,1024]{1,0:T(1,128)S(1)}) custom-call(s32[2,528]{1,0:T(2,128)S(1)} %bitcast.1, bf16[2,32,64,512]{3,2,1,0:T(8,128)(2,1)} %volt_ref.1), custom_call_target="tpu_custom_call" | custom-call | tf_op jit(solution)/shard_map/corner_turn/pallas_call | solution.py:190
  100.7 6.9 %tile_placement.1 = f32[528,1,64,128]{3,2,1,0:T(8,128)} custom-call(s32[1,1024]{1,0:T(1,128)S(1)} %get-tuple-element.9.slots_ref, bf16[2,1,2048,512]{3,2,1,0:T(8,128)(2,1)S(1)} %get-tuple-element.10.turned_ref, bf16[8,2,512,512]{3,2,1,0:T(8,128)(2,1)S(1)} %get-tuple-element.11.right_ref, f32[28,16,64,128]{3,2,1,0:T(8,128)S(1)} %get-tuple-element.12.tiles_ref), custom_call_target="tpu_custom_call" | custom-call | tf_op jit(solution)/shard_map/tile_placement/pallas_call | solution.py:211
Async XLA Ops:
  0.0 0.7 copy-start

commit v3 on v2

--- a/solution.py
+++ b/solution.py
@@ -34,16 +34,18 @@
 
 def send_order(sizes):
     half = sizes[1] // 2
-    order = []
-    for chan_mask in range(sizes[0]):
-        for tile_mask in range(half):
-            order.append((chan_mask, tile_mask + half))
-            if chan_mask or tile_mask:
-                order.append((chan_mask, tile_mask))
+    masks = [(chan_mask, tile_mask) for chan_mask in range(sizes[0]) for tile_mask in range(half)]
+    near, far = masks[1:], [(chan_mask, tile_mask + half) for chan_mask, tile_mask in masks]
+    order, nears = [], 0
+    for fars in range(len(far)):
+        order.append(far[fars])
+        while nears < len(near) and 2 * nears < 3 * (fars + 1):
+            order.append(near[nears])
+            nears += 1
     return order
 
 
-def multiply(turned_ref, right_ref, store, g, h, width):
+def multiply(turned_ref, right_ref, g, h, width):
     spectra = turned_ref.shape[3]
     rows = pl.ds(pl.multiple_of(g * width, width), width)
     total = None
@@ -57,13 +59,17 @@
         total = term if total is None else total + term
     total = total * spectra ** (-0.5)
     per = width // PANEL
-    for m in range(per):
-        for q in range(per):
-            store(m * per + q, total[m * PANEL : (m + 1) * PANEL, q * 2 * PANEL : (q + 1) * 2 * PANEL])
+    return jnp.stack(
+        [
+            total[m * PANEL : (m + 1) * PANEL, q * 2 * PANEL : (q + 1) * 2 * PANEL]
+            for m in range(per)
+            for q in range(per)
+        ]
+    )
 
 
 def turn_kernel(
-    sizes, pairs_ref, volt_ref, turned_ref, right_ref, tiles_ref, slots_ref, send_sem, recv_sem, own_sem
+    sizes, pairs_hbm, volt_ref, turned_ref, right_ref, tiles_ref, slots_ref, pairs_ref, send_sem, recv_sem, own_sem
 ):
     chan, tile = lax.axis_index("chan"), lax.axis_index("tile")
     me = chan * sizes[1] + tile
@@ -72,17 +78,21 @@
     width = turned_ref.shape[2] // groups
     per = width // PANEL
     order = send_order(sizes)
+    chans = [flipped(chan, mask, sizes[0]) for mask in range(sizes[0])]
+    tiles = [flipped(tile, mask, sizes[1]) for mask in range(sizes[1])]
 
     barrier = pltpu.get_barrier_semaphore()
     for masks in order:
-        to = (flipped(chan, masks[0], sizes[0]), flipped(tile, masks[1], sizes[1]))
+        to = (chans[masks[0]], tiles[masks[1]])
         pl.semaphore_signal(barrier, inc=1, device_id=to, device_id_type=MESH)
+    fetch = pltpu.make_async_copy(pairs_hbm, pairs_ref, own_sem.at[1])
+    fetch.start()
     pl.semaphore_wait(barrier, len(order))
 
     rows = pl.ds(pl.multiple_of(me * inputs, inputs), inputs)
     copies = {}
     for number, masks in enumerate(order):
-        to = (flipped(chan, masks[0], sizes[0]), flipped(tile, masks[1], sizes[1]))
+        to = (chans[masks[0]], tiles[masks[1]])
         copies[masks] = pltpu.make_async_remote_copy(
             src_ref=volt_ref.at[:, pl.ds(to[0] * sizes[1] + to[1], 1)],
             dst_ref=turned_ref.at[:, :, rows],
@@ -92,9 +102,10 @@
             device_id_type=MESH,
         )
         copies[masks].start()
-    own = pltpu.make_async_copy(volt_ref.at[:, pl.ds(me, 1)], turned_ref.at[:, :, rows], own_sem)
+    own = pltpu.make_async_copy(volt_ref.at[:, pl.ds(me, 1)], turned_ref.at[:, :, rows], own_sem.at[0])
     own.start()
 
+    fetch.wait()
     listed = pairs_ref.shape[1]
     code = pairs_ref[0:1, :] * PANELS + pairs_ref[1:2, :]
     code = jnp.transpose(jnp.broadcast_to(code, (128, listed)))
@@ -111,25 +122,17 @@
             if masks[0] * 2 + masks[1] // (sizes[1] // 2) == place:
                 copies[masks].wait_recv()
         x = group_at(sizes, chan, tile, place)
-        for q in range(per):
-            panel = pl.ds(pl.multiple_of(x * width + q * PANEL, PANEL), PANEL)
-            real_part = turned_ref[0, 0, panel, :]
-            imag_part = turned_ref[1, 0, panel, :]
-            first, second = pl.ds(q * 2 * PANEL, PANEL), pl.ds(q * 2 * PANEL + PANEL, PANEL)
-            right_ref[x, 0, first, :] = real_part
-            right_ref[x, 0, second, :] = -imag_part
-            right_ref[x, 1, first, :] = imag_part
-            right_ref[x, 1, second, :] = real_part
+        rows = pl.ds(pl.multiple_of(x * width, width), width)
+        real_part, imag_part = turned_ref[0, 0, rows, :], turned_ref[1, 0, rows, :]
+        cut = [slice(q * PANEL, (q + 1) * PANEL) for q in range(per)]
+        right_ref[x, 0] = jnp.concatenate([piece for c in cut for piece in (real_part[c], -imag_part[c])], axis=0)
+        right_ref[x, 1] = jnp.concatenate([piece for c in cut for piece in (imag_part[c], real_part[c])], axis=0)
         if place < groups - LATE:
 
             def block(other, carry):
                 y = group_at(sizes, chan, tile, other)
                 at = jnp.where(other == place, pair_index(0, groups - LATE) + place, pair_index(other, place))
-
-                def store(number, value):
-                    tiles_ref[at, number] = value
-
-                multiply(turned_ref, right_ref, store, jnp.minimum(x, y), jnp.maximum(x, y), width)
+                tiles_ref[at] = multiply(turned_ref, right_ref, jnp.minimum(x, y), jnp.maximum(x, y), width)
                 return carry
 
             lax.fori_loop(0, place + 1, block, 0)
@@ -138,7 +141,9 @@
         copies[masks].wait_send()
 
 
-def place_kernel(sizes, slots_ref, turned_ref, right_ref, tiles_ref, out_ref, last_ref, sem):
+def place_kernel(sizes, slots_vmem, turned_ref, right_ref, tiles_ref, out_ref, last_ref, slots_ref, slots_sem, sem):
+    fetch = pltpu.make_async_copy(slots_vmem, slots_ref, slots_sem)
+    fetch.start()
     chan, tile = lax.axis_index("chan"), lax.axis_index("tile")
     groups = 2 * sizes[0]
     width = turned_ref.shape[2] // groups
@@ -159,15 +164,13 @@
     late = [(a, b) for b in range(early, groups) for a in range(b + 1)]
     share = -(-len(ready) // len(late))
     for number, (a, b) in enumerate(late):
+        last_ref[number] = multiply(
+            turned_ref, right_ref, jnp.minimum(ids[a], ids[b]), jnp.maximum(ids[a], ids[b]), width
+        )
+        if number == 0:
+            fetch.wait()
         for k in range(number * share, min((number + 1) * share, len(ready))):
             put(tiles_ref.at[k], ids[ready[k][0]], ids[ready[k][1]])
-
-        def store(place, value):
-            last_ref[number, place] = value
-
-        multiply(
-            turned_ref, right_ref, store, jnp.minimum(ids[a], ids[b]), jnp.maximum(ids[a], ids[b]), width
-        )
         put(last_ref.at[number], ids[a], ids[b])
 
     def drain(index, carry):
@@ -195,26 +198,32 @@
             pltpu.VMEM((early * (early + 1) // 2, per * per, PANEL, 2 * PANEL), jnp.float32),
             pltpu.VMEM((1, PANELS * PANELS), jnp.int32),
         ),
-        in_specs=[vmem, pl.BlockSpec(memory_space=pltpu.HBM)],
+        in_specs=[pl.BlockSpec(memory_space=pltpu.HBM)] * 2,
         out_specs=(vmem,) * 4,
         scratch_shapes=[
+            pltpu.VMEM((2, listed), jnp.int32),
             pltpu.SemaphoreType.DMA((devices - 1,)),
             pltpu.SemaphoreType.DMA((devices - 1,)),
-            pltpu.SemaphoreType.DMA,
+            pltpu.SemaphoreType.DMA((2,)),
         ],
         compiler_params=pltpu.CompilerParams(
             collective_id=0, has_side_effects=True, vmem_limit_bytes=12 * MIB
         ),
         name="corner_turn",
-    )(tile_pairs.T, pltpu.with_memory_space_constraint(voltages, pltpu.HBM))
+    )(
+        pltpu.with_memory_space_constraint(tile_pairs.T, pltpu.HBM),
+        pltpu.with_memory_space_constraint(voltages, pltpu.HBM),
+    )
     turned, right, tiles, slots = results
     return pl.pallas_call(
         functools.partial(place_kernel, sizes),
         out_shape=jax.ShapeDtypeStruct((listed, 1, PANEL, 2 * PANEL), jnp.float32),
-        in_specs=[pl.BlockSpec(memory_space=pltpu.SMEM), vmem, vmem, vmem],
+        in_specs=[vmem] * 4,
         out_specs=pl.BlockSpec(memory_space=pl.ANY),
         scratch_shapes=[
             pltpu.VMEM((groups * LATE - LATE * (LATE - 1) // 2, per * per, PANEL, 2 * PANEL), jnp.float32),
+            pltpu.SMEM((1, PANELS * PANELS), jnp.int32),
+            pltpu.SemaphoreType.DMA,
             pltpu.SemaphoreType.DMA,
         ],
         compiler_params=pltpu.CompilerParams(vmem_limit_bytes=16 * MIB),

time: 108 us -> 106 us (0.981)
  no operation moved by 1% of the time
where the time goes in v3:
time: 106 us
  Pallas kernels  106 us (100%)
    pallas_call x1, Pallas kernels, body(): pl.pallas_call(functools.partial(turn_kernel, sizes), out_shape=(pltpu.VM...  99.3 us
    pallas_call x1, Pallas kernels, body(): pl.pallas_call(functools.partial(place_kernel, sizes), out_shape=jax.Shap...  6.67 us

profile of v3, /device:TPU:9, one launch (start us, length us, event | category | flops | bytes accessed | tf_op | source)
XLA Modules:
  0.0 106.0 jit_solution(5921495408462970447)
XLA Ops:
  0.0 99.3 %corner_turn.1 = (bf16[2,1,2048,512]{3,2,1,0:T(8,128)(2,1)S(1)}, bf16[8,2,512,512]{3,2,1,0:T(8,128)(2,1)S(1)}, f32[28,16,64,128]{3,2,1,0:T(8,128)S(1)}, s32[1,1024]{1,0:T(1,128)S(1)}) custom-call(s32[2,528]{1,0:T(2,128)} %bitcast.1, bf16[2,32,64,512]{3,2,1,0:T(8,128)(2,1)} %volt_ref.1), custom_call_target="tpu_custom_call" | custom-call | tf_op jit(solution)/shard_map/corner_turn/pallas_call | solution.py:193
  99.3 6.7 %tile_placement.1 = f32[528,1,64,128]{3,2,1,0:T(8,128)} custom-call(s32[1,1024]{1,0:T(1,128)S(1)} %get-tuple-element.9.slots_vmem, bf16[2,1,2048,512]{3,2,1,0:T(8,128)(2,1)S(1)} %get-tuple-element.10.turned_ref, bf16[8,2,512,512]{3,2,1,0:T(8,128)(2,1)S(1)} %get-tuple-element.11.right_ref, f32[28,16,64,128]{3,2,1,0:T(8,128)S(1)} %get-tuple-element.12.tiles_ref), custom_call_target="tpu_custom_call" | custom-call | tf_op jit(solution)/shard_map/tile_placement/pallas_call | solution.py:218

commit v4 on v3

--- a/solution.py
+++ b/solution.py
@@ -32,16 +32,14 @@
     return count(b) + a
 
 
-def send_order(sizes):
+def send_order(sizes, lead):
     half = sizes[1] // 2
     masks = [(chan_mask, tile_mask) for chan_mask in range(sizes[0]) for tile_mask in range(half)]
     near, far = masks[1:], [(chan_mask, tile_mask + half) for chan_mask, tile_mask in masks]
-    order, nears = [], 0
-    for fars in range(len(far)):
-        order.append(far[fars])
-        while nears < len(near) and 2 * nears < 3 * (fars + 1):
-            order.append(near[nears])
-            nears += 1
+    order = []
+    for number, masks in enumerate(far):
+        order.append(masks)
+        order += near[number * lead : (number + 1) * lead]
     return order
 
 
@@ -77,7 +75,7 @@
     groups = 2 * sizes[0]
     width = turned_ref.shape[2] // groups
     per = width // PANEL
-    order = send_order(sizes)
+    order = send_order(sizes, 1)
     chans = [flipped(chan, mask, sizes[0]) for mask in range(sizes[0])]
     tiles = [flipped(tile, mask, sizes[1]) for mask in range(sizes[1])]
 
@@ -101,7 +99,19 @@
             device_id=to,
             device_id_type=MESH,
         )
-        copies[masks].start()
+
+    middle = (tile // (sizes[1] // 2) + tile // (sizes[1] // 4)) % 2
+
+    @pl.when(middle == 1)
+    def _():
+        for masks in order:
+            copies[masks].start()
+
+    @pl.when(middle == 0)
+    def _():
+        for masks in send_order(sizes, 2):
+            copies[masks].start()
+
     own = pltpu.make_async_copy(volt_ref.at[:, pl.ds(me, 1)], turned_ref.at[:, :, rows], own_sem.at[0])
     own.start()
 

time: 106 us -> 106 us (level); the launches traced: 106 us -> 105 us
    pallas_call x1, Pallas kernels: 99.3 us -> 97.9 us  [body(): pl.pallas_call(functools.partial(turn_kernel, sizes), out_shape=(pltpu.VM...]
where the time goes in v4:
time: 106 us; the launch traced here: 105 us
  Pallas kernels  105 us (99%)
    pallas_call x1, Pallas kernels, body(): pl.pallas_call(functools.partial(turn_kernel, sizes), out_shape=(pltpu.VM...  97.9 us
    pallas_call x1, Pallas kernels, body(): pl.pallas_call(functools.partial(place_kernel, sizes), out_shape=jax.Shap...  6.67 us

profile of v4, /device:TPU:9, one launch (start us, length us, event | category | flops | bytes accessed | tf_op | source)
XLA Modules:
  0.0 104.6 jit_solution(10489090479249281715)
XLA Ops:
  0.0 97.9 %corner_turn.1 = (bf16[2,1,2048,512]{3,2,1,0:T(8,128)(2,1)S(1)}, bf16[8,2,512,512]{3,2,1,0:T(8,128)(2,1)S(1)}, f32[28,16,64,128]{3,2,1,0:T(8,128)S(1)}, s32[1,1024]{1,0:T(1,128)S(1)}) custom-call(s32[2,528]{1,0:T(2,128)} %bitcast.1, bf16[2,32,64,512]{3,2,1,0:T(8,128)(2,1)} %volt_ref.1), custom_call_target="tpu_custom_call" | custom-call | tf_op jit(solution)/shard_map/corner_turn/pallas_call | solution.py:203
  97.9 6.7 %tile_placement.1 = f32[528,1,64,128]{3,2,1,0:T(8,128)} custom-call(s32[1,1024]{1,0:T(1,128)S(1)} %get-tuple-element.9.slots_vmem, bf16[2,1,2048,512]{3,2,1,0:T(8,128)(2,1)S(1)} %get-tuple-element.10.turned_ref, bf16[8,2,512,512]{3,2,1,0:T(8,128)(2,1)S(1)} %get-tuple-element.11.right_ref, f32[28,16,64,128]{3,2,1,0:T(8,128)S(1)} %get-tuple-element.12.tiles_ref), custom_call_target="tpu_custom_call" | custom-call | tf_op jit(solution)/shard_map/tile_placement/pallas_call | solution.py:228
